TPU v7x, 32 devices: a whole 2x2x4 slice. The times are simulated.
32 devices in a mesh: seq: 8 (over y, x, core), head: 4 (over z).
Axes of the slice: x: 2, y: 2, z: 4, core: 2. Of those that a mesh axis runs over, the one named last changes fastest.
Arguments:
- tokens: bfloat16 [2, 8192, 2048], P(None, ('seq', 'head')), may hold values from -6 to 6
- norm_gain: float32 [2048], replicated, may hold values from 0.25 to 1.75
- projection: bfloat16 [2048, 6144], P(None, 'head'), may hold values from -0.125 to 0.125
- level_table: float32 [16, 16, 18], P(None, 'head'), may hold values from 0.05 to 1
- level_index: int32 [2, 8192], P(None, 'seq'), may hold values from 0 to 15
- lengths: int32 [2], replicated, may hold values from 4096 to 8192, as said below
Outputs:
- attended: bfloat16 [2, 8192, 2048], P(None, 'seq', 'head')
Inputs may be any that keep to these rules, and one draw needn't show every extreme that they name: The first sequence is always whole: lengths[0] = 8192.
All inputs are finite; a program needn't handle non-finite values.
Results may differ from a plain program's by a relative error of at most 0.0097.
Values may be sent and summed in bfloat16 or wider, within the bound.
A program may use at most 128 MiB of HBM per device.

v0:
```python
import jax
import jax.numpy as jnp
from jax import lax
from jax.sharding import PartitionSpec as P

SPAN = 512


def swapped(array, axis, bit):
    return lax.ppermute(array, axis, [(i, i ^ 1 << bit) for i in range(lax.axis_size(axis))])


def digit_count(values, limit):
    counted = jnp.zeros(values.shape, jnp.int32)
    for shift in range(limit):
        counted = counted + (values >= 1 << shift).astype(jnp.int32)
    return counted


def on_device(tokens, norm_gain, projection, level_table, level_index, lengths):
    batch_seqs, row_count, model_width = tokens.shape
    heads_here = level_table.shape[1]
    head_size = projection.shape[1] // (3 * heads_here)
    widened = tokens.astype(jnp.float32)
    normed = (
        widened * lax.rsqrt(jnp.mean(widened * widened, -1, keepdims=True) + 1e-06) * norm_gain
    ).astype(jnp.bfloat16)
    groups = lax.axis_size("head")
    block_len = row_count * groups
    block_rows = lax.all_gather(normed, "head", axis=1, tiled=True)
    projected_here = jnp.einsum(
        "srd,dc->src", block_rows, projection, preferred_element_type=jnp.float32
    )
    projected_here = projected_here.astype(jnp.bfloat16).reshape(
        batch_seqs, block_len, heads_here, 3, head_size
    )
    span_count = block_len // SPAN
    local_bits = span_count.bit_length() - 1
    lchunk = SPAN.bit_length() - 1
    table_count = level_table.shape[0]
    level_total = level_table.shape[2]
    onehot = (level_index[..., None] == jnp.arange(table_count, dtype=jnp.int32)).astype(
        jnp.float32
    )
    weights = jnp.einsum("stg,ghl->sthl", onehot, level_table, precision=lax.Precision.HIGHEST)
    weights = weights.reshape(batch_seqs, span_count, SPAN, heads_here, level_total)
    shaped = projected_here.reshape(batch_seqs, span_count, SPAN, heads_here, 3, head_size)
    queries = shaped[:, :, :, :, 0]
    keys_here = shaped[:, :, :, :, 1]
    values_here = shaped[:, :, :, :, 2]
    positions = jnp.arange(SPAN, dtype=jnp.int32)
    level_grid = digit_count(jnp.bitwise_xor(positions[:, None], positions[None, :]), lchunk + 1)
    causal = (positions[:, None] >= positions[None, :]).astype(jnp.float32)
    scores = jnp.einsum(
        "scthd,scuhd->schtu", queries, keys_here, preferred_element_type=jnp.float32
    )
    head_weights = weights.transpose(0, 1, 3, 2, 4)
    grid = jnp.zeros(scores.shape, jnp.float32)
    for level_step in range(lchunk + 1):
        grid = grid + head_weights[..., level_step][..., None] * (level_grid == level_step).astype(
            jnp.float32
        )
    weighted = (scores * grid * causal).astype(jnp.bfloat16)
    near_part = jnp.einsum(
        "schtu,scuhe->scthe", weighted, values_here, preferred_element_type=jnp.float32
    )
    states = jnp.einsum(
        "scthd,scthe->schde", keys_here, values_here, preferred_element_type=jnp.float32
    )
    totals = jnp.sum(states, axis=1)
    span_ids = jnp.arange(span_count, dtype=jnp.int32)
    span_dist = digit_count(jnp.bitwise_xor(span_ids[:, None], span_ids[None, :]), local_bits + 1)
    span_earlier = span_ids[None, :] < span_ids[:, None]
    level_step = 0
    span_mask = ((span_dist == level_step + 1) & span_earlier).astype(jnp.float32)
    bucket = jnp.einsum(
        "cb,sbhde->schde", span_mask, states, precision=lax.Precision.HIGHEST
    ).astype(jnp.bfloat16)
    readout = jnp.einsum("scthd,schde->scthe", queries, bucket, preferred_element_type=jnp.float32)
    far_part = weights[..., lchunk + 1 + level_step][..., None] * readout
    own_index = lax.axis_index("seq")
    seq_bits = lax.axis_size("seq").bit_length() - 1
    block_sum = totals
    sibling_list = []
    for level_bit in range(seq_bits):
        sibling = swapped(block_sum, "seq", level_bit)
        upper_half = own_index // (1 << level_bit) % 2 == 1
        sibling_list.append(jnp.where(upper_half, sibling, 0.0))
        block_sum = block_sum + sibling
    far_buckets = jnp.stack(sibling_list)
    for level_step in range(seq_bits):
        bucket = far_buckets[level_step].astype(jnp.bfloat16)
        readout = jnp.einsum(
            "scthd,shde->scthe", queries, bucket, preferred_element_type=jnp.float32
        )
        far_part = (
            far_part + weights[..., lchunk + local_bits + 1 + level_step][..., None] * readout
        )
    output = near_part + far_part
    output = output * lax.rsqrt(jnp.mean(output * output, -1, keepdims=True) + 1e-06)
    output = output.reshape(batch_seqs, block_len, heads_here * head_size)
    global_pos = own_index * block_len + jnp.arange(block_len, dtype=jnp.int32)
    valid = global_pos[None, :] < lengths[:, None]
    return jnp.where(valid[..., None], output, 0.0).astype(jnp.bfloat16)


def solution(mesh):
    in_specs = (
        P(None, ("seq", "head"), None),
        P(),
        P(None, "head"),
        P(None, "head", None),
        P(None, "seq"),
        P(),
    )
    out_specs = P(None, "seq", "head")
    return jax.shard_map(
        on_device, mesh=mesh, in_specs=in_specs, out_specs=out_specs, check_vma=False
    )
```

profile of v0, /device:TPU:0, one launch (start us, length us, event | category | flops | bytes accessed | tf_op | source)
XLA Modules:
  0.0 295.8 jit_solution(17000002026639026044)
XLA Ops:
  6.5 2.1 fusion.8
  8.6 3.5 %fusion.10 = bf16[2,256,2048]{2,1,0:T(8,128)(2,1)} fusion(bf16[2,256,2048]{2,1,0:T(8,128)(2,1)} %param.6, f32[2048]{0:T(1024)} %param.7, f32[2,256]{1,0:T(2,128)S(1)} %add_rsqrt_fusion.1), kind=kLoop, calls=%fused_computation.10 | loop fusion | flops 4194304 | bytes 4204544 | tf_op jit(solution)/shard_map/convert_element_type | solution.py:27
  12.1 0.0 all-gather.2.cloned.1.call-update
  12.2 0.5 fusion.55
  12.7 0.5 reshape.220
  13.2 0.3 copy.114
  13.6 0.6 copy.81
  14.2 0.6 copy.85
  15.1 0.3 compare_convert_fusion.9
  15.3 0.4 compare_convert_fusion.7
  15.7 0.0 copy-start.8
  15.7 1.7 compare_convert_fusion.5
  17.5 1.8 compare_convert_fusion.3
  19.2 1.8 compare_convert_fusion.1
  21.0 1.7 fusion.40
  22.7 0.0 copy-done.8
  22.7 0.1 broadcast_compare_fusion
  22.8 141.8 %all-gather.2.cloned.1.call-done = bf16[2,1024,2048]{2,1,0:T(8,128)(2,1)} async-done(((bf16[2,256,2048]{2,1,0:T(8,128)(2,1)}), bf16[2,1024,2048]{2,1,0:T(8,128)(2,1)}) %all-gather.2.cloned.1.call-update) | async-done | bytes 8388624 | tf_op jit(solution)/shard_map/all_gather | solution.py:30
  164.6 18.6 %fusion.5 = bf16[2,1024,1536]{2,1,0:T(8,128)(2,1)} fusion(bf16[2,1024,2048]{2,1,0:T(8,128)(2,1)} %all-gather.2.cloned.1.call-done, bf16[2048,1536]{1,0:T(8,128)(2,1)} %param.8), kind=kOutput, calls=%fused_computation.5 | convolution fusion | flops 12888047616 | bytes 20971520 | tf_op jit(solution)/shard_map/srd,dc->src/dot_general | solution.py:31
  183.2 8.7 %copy.60 = bf16[2,1024,1536]{1,2,0:T(8,128)(2,1)} copy(bf16[2,1024,1536]{2,1,0:T(8,128)(2,1)} %fusion.5) | data formatting | bytes 12582912 | tf_op jit(solution)/shard_map/convert_element_type | solution.py:34
  191.9 11.1 %reshape_reshape.3 = bf16[2,2,512,4,3,128]{2,1,5,4,3,0:T(2,128)(2,1)} reshape(bf16[2,1024,1536]{1,2,0:T(8,128)(2,1)} %copy.60) | data formatting | bytes 12582912 | tf_op jit(solution)/shard_map/reshape;reshape | solution.py:47
  203.1 7.6 %fusion.75 = (bf16[2,2,512,4,1,128]{2,1,5,4,3,0:T(2,128)(2,1)}, bf16[2,2,512,4,1,128]{2,1,5,4,3,0:T(2,128)(2,1)}, bf16[2,2,512,4,1,128]{2,1,5,4,3,0:T(2,128)(2,1)}) fusion(bf16[2,2,512,4,3,128]{2,1,5,4,3,0:T(2,128)(2,1)} %reshape_reshape.3), kind=kLoop, calls=%fused_computation.116 | loop fusion | bytes 12582912 | tf_op jit(solution)/shard_map/slice | solution.py:50
  210.7 6.2 %copy.97 = bf16[2,2,512,4,1,128]{5,2,3,1,0,4:T(8,128)(2,1)} copy(bf16[2,2,512,4,1,128]{2,1,5,4,3,0:T(2,128)(2,1)} %get-tuple-element.6) | data formatting | bytes 4194304
  216.9 4.9 %fusion.77 = (f32[2,4,128,128]{3,2,1,0:T(8,128)}, f32[2,2,4,128,128]{4,3,2,1,0:T(8,128)}) fusion(bf16[2,2,512,4,1,128]{2,1,5,4,3,0:T(2,128)(2,1)} %get-tuple-element.5, bf16[2,2,512,4,1,128]{5,2,3,1,0,4:T(8,128)(2,1)} %copy.97), kind=kOutput, calls=%fused_computation.118 | convolution fusion | flops 268566528 | bytes 5767168 | tf_op jit(solution)/shard_map/scthd,scthe->schde/dot_general | solution.py:67
  221.8 2.1 copy.82
  223.8 0.1 collective-permute-start
  223.9 6.2 %copy.96 = bf16[2,2,512,4,1,128]{5,2,3,1,0,4:T(8,128)(2,1)} copy(bf16[2,2,512,4,1,128]{2,1,5,4,3,0:T(2,128)(2,1)} %get-tuple-element.7) | data formatting | bytes 4194304
  230.1 20.1 %multiply_convert_fusion.4 = bf16[2,2,4,512,512]{4,3,2,1,0:T(8,128)(2,1)S(1)} fusion(f32[512,512]{1,0:T(8,128)} %get-tuple-element.28, f32[512,512]{1,0:T(8,128)} %get-tuple-element.29, f32[2,2,4,512]{3,2,1,0:T(4,128)S(1)} %copy.75, f32[512,512]{1,0:T(8,128)} %get-tuple-element.30, f32[2,2,4,512]{3,2,1,0:T(4,128)S(1)} %copy.74, ...), kind=kOutput, calls=%fused_computation.clone.clone.1 | convolution fusion | flops 1166016512 | bytes 24444928 | tf_op jit(solution)/shard_map/scthd,scuhd->schtu/dot_general | solution.py:54
  250.2 2.8 fusion
  253.1 0.0 copy-start
  253.1 0.0 copy-done.3
  253.1 2.6 fusion.28
  255.7 0.0 collective-permute-done
  255.7 1.1 add.587
  256.8 1.5 collective-permute-start.1
  258.3 0.8 fusion.24
  259.1 0.7 fusion.22
  259.8 11.3 %collective-permute-done.1 = f32[2,4,128,128]{2,3,1,0:T(8,128)S(1)} collective-permute-done((f32[2,4,128,128]{2,3,1,0:T(8,128)S(1)}, f32[2,4,128,128]{2,3,1,0:T(8,128)S(1)}, u32[]{:S(2)}, u32[]{:S(2)}) %collective-permute-start.1) | collective-permute-done | bytes 524320 | tf_op jit(solution)/shard_map/ppermute | solution.py:10
  271.2 0.1 add.590
  271.2 1.5 collective-permute-start.2
  272.8 0.7 fusion.20
  273.5 5.7 %collective-permute-done.2 = bf16[2,4,128,128]{2,3,1,0:T(8,128)(2,1)S(1)} collective-permute-done((bf16[2,4,128,128]{2,3,1,0:T(8,128)(2,1)S(1)}, bf16[2,4,128,128]{2,3,1,0:T(8,128)(2,1)S(1)}, u32[]{:S(2)}, u32[]{:S(2)}) %collective-permute-start.2) | collective-permute-done | bytes 262176 | tf_op jit(solution)/shard_map/ppermute | solution.py:10
  279.2 0.0 copy-done.4
  279.2 2.1 multiply_reduce_fusion
  281.3 0.6 broadcast_multiply_fusion
  282.0 2.5 copy.86
  284.5 2.7 reshape.212
  287.3 1.7 select_convert_fusion
  (31 shorter events, 0.2 us)
Async XLA Ops:
  6.5 5.7 %copy-start.7 = (s32[2,1024]{1,0:T(2,128)S(1)}, s32[2,1024]{1,0:T(2,128)}, u32[]{:S(2)}) copy-start(s32[2,1024]{1,0:T(2,128)} %param.10) | copy-start | bytes 24580
  6.5 5.7 %copy-start.6 = (f32[16,4,18]{2,1,0:T(4,128)S(1)}, f32[16,4,18]{2,1,0:T(4,128)}, u32[]{:S(2)}) copy-start(f32[16,4,18]{2,1,0:T(4,128)} %param.9) | copy-start | bytes 13828
  6.5 158.1 %all-gather.2.cloned.1.call-start = ((), (), s32[]{:S(2)}) async-start(), calls=%async_computation | async-start | bytes 10485760 | tf_op jit(solution)/shard_map/all_gather | solution.py:30
  15.7 7.0 %copy-start.8 = (s32[2]{0:T(128)S(1)}, s32[2]{0:T(128)}, u32[]{:S(2)}) copy-start(s32[2]{0:T(128)} %param.11) | copy-start | bytes 28
  223.8 31.9 %collective-permute-start = (f32[2,4,128,128]{2,3,1,0:T(8,128)}, f32[2,4,128,128]{2,3,1,0:T(8,128)}, u32[]{:S(2)}, u32[]{:S(2)}) collective-permute-start(f32[2,4,128,128]{2,3,1,0:T(8,128)} %copy.82), channel_id=1, source_target_pairs={{0,4},{4,0},{8,12},{12,8},{16,20},{20,16},{24,28},{28,24},{1,5},{5... | collective-permute-start | bytes 1572872 | tf_op jit(solution)/shard_map/ppermute | solution.py:10
  230.1 20.1 %copy-start.1 = (bf16[2,2,512,4,1,128]{2,1,5,4,3,0:T(2,128)(2,1)S(1)}, bf16[2,2,512,4,1,128]{2,1,5,4,3,0:T(2,128)(2,1)}, u32[]{:S(2)}) copy-start(bf16[2,2,512,4,1,128]{2,1,5,4,3,0:T(2,128)(2,1)} %get-tuple-element.5) | copy-start | bytes 6291460
  250.2 2.9 copy-start.3
  250.2 5.5 %copy-start.2 = (f32[2,4,128,128]{2,3,1,0:T(8,128)S(1)}, f32[2,4,128,128]{2,3,1,0:T(8,128)}, u32[]{:S(2)}) copy-start(f32[2,4,128,128]{2,3,1,0:T(8,128)} %copy.82) | copy-start | bytes 1572868
  253.1 5.3 %copy-start = (bf16[2,2,512,4,1,128]{5,2,3,1,0,4:T(8,128)(2,1)S(1)}, bf16[2,2,512,4,1,128]{5,2,3,1,0,4:T(8,128)(2,1)}, u32[]{:S(2)}) copy-start(bf16[2,2,512,4,1,128]{5,2,3,1,0,4:T(8,128)(2,1)} %copy.96) | copy-start | bytes 6291460
  256.8 14.3 %collective-permute-start.1 = (f32[2,4,128,128]{2,3,1,0:T(8,128)S(1)}, f32[2,4,128,128]{2,3,1,0:T(8,128)S(1)}, u32[]{:S(2)}, u32[]{:S(2)}) collective-permute-start(f32[2,4,128,128]{2,3,1,0:T(8,128)S(1)} %add.587), channel_id=1, source_target_pairs={{0,8},{4,12},{8,0},{12,4},{16,24},{20,28},{24,16},{28,20},{1,9},{5... | collective-permute-start | bytes 1572872 | tf_op jit(solution)/shard_map/ppermute | solution.py:10
  259.8 19.3 %copy-start.4 = (f32[2,2,512,4]{2,3,1,0:T(4,128)S(1)}, f32[2,2,512,4]{2,3,1,0:T(4,128)}, u32[]{:S(2)}) copy-start(f32[2,2,512,4]{2,3,1,0:T(4,128)} %copy.81) | copy-start | bytes 98308
  259.8 19.3 %copy-start.5 = (f32[2,2,512,4]{2,3,1,0:T(4,128)S(1)}, f32[2,2,512,4]{2,3,1,0:T(4,128)}, u32[]{:S(2)}) copy-start(f32[2,2,512,4]{2,3,1,0:T(4,128)} %copy.85) | copy-start | bytes 98308
  271.2 7.9 %collective-permute-start.2 = (bf16[2,4,128,128]{2,3,1,0:T(8,128)(2,1)S(1)}, bf16[2,4,128,128]{2,3,1,0:T(8,128)(2,1)S(1)}, u32[]{:S(2)}, u32[]{:S(2)}) collective-permute-start(bf16[2,4,128,128]{2,3,1,0:T(8,128)(2,1)S(1)} %add.590), channel_id=1, source_target_pairs={{0,16},{4,20},{8,24},{12,28},{16,0},{20,4},{24,8},{28,12},{1,17},{... | collective-permute-start | bytes 786440 | tf_op jit(solution)/shard_map/ppermute | solution.py:10
Sparse Core Ops, SparseCore 0:
  12.3 152.3 all-gather.1
where the time goes:
time: 297 us; the launch traced here: 296 us
  waiting for transfers between devices  159 us (54%)
  matrix products  53.9 us (18%)
  local copies, waits for them, and re-layouts  49.4 us (17%)
  other arithmetic  16.7 us (6%)
  between operations  13.8 us (5%)
  starting transfers between devices  3.12 us (1%)
    all_gather x1, waiting for transfers between devices, on_device(): block_rows = lax.all_gather(normed, 'head', axis=1, tiled=True)  142 us
    dot_general x1, matrix products, on_device(): jnp.einsum('scthd,scuhd->schtu', queries, keys_here, preferred_element_ty...  20.1 us
    dot_general x1, matrix products, on_device(): jnp.einsum('srd,dc->src', block_rows, projection, preferred_element_type=...  18.6 us
    ppermute x3, waiting for transfers between devices, swapped(): lax.ppermute(array, axis, [(i, i ^ 1 << bit) for i in range(lax.axis_size...  17 us
    unnamed x20, local copies, waits for them, and re-layouts  12.4 us
    another operation x1, local copies, waits for them, and re-layouts, on_device(): projected_here.reshape(batch_seqs, span_count, SPAN, heads_here, 3, head_...  11.1 us
    convert_element_type x1, local copies, waits for them, and re-layouts, on_device(): projected_here.astype(jnp.bfloat16)  8.69 us
    slice x1, local copies, waits for them, and re-layouts, on_device(): values_here = shaped[:, :, :, :, 2]  7.6 us
  transfers between devices with their start and end apart: 4, of which 3 were waited for; matrix products, arithmetic and copies ran while one was open for 15% of the time, Pallas kernels for 0%

commit v1 on v0

v1 whole, which is shorter than its diff:
```python
import functools

import jax
import jax.numpy as jnp
from jax import lax
from jax.experimental import pallas as pl
from jax.experimental.pallas import tpu as pltpu
from jax.sharding import PartitionSpec as P

SPAN = 512
LANE = 128
STRIDE = 32
VMEM_LIMIT = 56 * 1024 * 1024
NT = (((1,), (1,)), ((), ()))
TN = (((0,), (0,)), ((), ()))


def swapped(array, axis, bit):
    return lax.ppermute(array, axis, [(i, i ^ 1 << bit) for i in range(lax.axis_size(axis))])


def dot32(a, b):
    return jnp.dot(a, b, preferred_element_type=jnp.float32)


def near_kernel(
    heads, head_size, rows_ref, gain_ref, proj_ref, weight_ref, q_ref, near_ref, total_ref, normed, qkv
):
    span = pl.program_id(0)
    lchunk = SPAN.bit_length() - 1

    @pl.when(span == 0)
    def _():
        total_ref[...] = jnp.zeros_like(total_ref)

    piece = 128
    for start in range(0, SPAN, piece):
        x = rows_ref[start : start + piece].astype(jnp.float32)
        scale = lax.rsqrt(jnp.mean(x * x, -1, keepdims=True) + 1e-06)
        normed[start : start + piece] = (x * scale * gain_ref[...]).astype(jnp.bfloat16)
    width = proj_ref.shape[1]
    step = 2 * 3 * head_size if width % (6 * head_size) == 0 else 3 * head_size
    for col in range(0, width, step):
        qkv[:, col : col + step] = dot32(normed[...], proj_ref[:, col : col + step]).astype(
            jnp.bfloat16
        )

    t = lax.broadcasted_iota(jnp.int32, (LANE, LANE), 0)
    u = lax.broadcasted_iota(jnp.int32, (LANE, LANE), 1)
    apart = t ^ u
    level = jnp.zeros((LANE, LANE), jnp.int32)
    for shift in range(LANE.bit_length() - 1):
        level = level + (apart >= 1 << shift).astype(jnp.int32)
    level = jnp.where(u <= t, level, STRIDE - 1)

    for h in range(heads):
        base = h * 3 * head_size
        q = qkv[:, base : base + head_size]
        k = qkv[:, base + head_size : base + 2 * head_size]
        v = qkv[:, base + 2 * head_size : base + 3 * head_size]
        out_cols = slice(h * head_size, (h + 1) * head_size)
        q_ref[:, out_cols] = q
        before = total_ref[h]
        readout = dot32(q, before.astype(jnp.bfloat16))
        for start in range(0, SPAN, LANE):
            rows = slice(start, start + LANE)
            w_rows = weight_ref[rows, :]
            grid = jnp.take_along_axis(w_rows, level + h * STRIDE, axis=1)
            scores = lax.dot_general(q[rows], k[rows], NT, preferred_element_type=jnp.float32)
            acc = dot32((scores * grid).astype(jnp.bfloat16), v[rows])
            far_at = h * STRIDE + lchunk + 1
            acc = acc + w_rows[:, far_at : far_at + 1] * readout[rows]
            size = LANE
            while size < SPAN:
                if start & size:
                    low = start & ~(2 * size - 1)
                    at = h * STRIDE + size.bit_length()
                    scores = lax.dot_general(
                        q[rows], k[low : low + size], NT, preferred_element_type=jnp.float32
                    )
                    scores = (scores * w_rows[:, at : at + 1]).astype(jnp.bfloat16)
                    acc = acc + dot32(scores, v[low : low + size])
                size *= 2
            near_ref[rows, out_cols] = acc
        total_ref[h] = before + lax.dot_general(k, v, TN, preferred_element_type=jnp.float32)


def near_call(rows, gain, projection, weights, heads, head_size):
    length, model_width = rows.shape
    width = projection.shape[1]
    out_width = heads * head_size
    return pl.pallas_call(
        functools.partial(near_kernel, heads, head_size),
        grid=(length // SPAN,),
        in_specs=[
            pl.BlockSpec((SPAN, model_width), lambda c: (c, 0)),
            pl.BlockSpec((1, model_width), lambda c: (0, 0)),
            pl.BlockSpec((model_width, width), lambda c: (0, 0)),
            pl.BlockSpec((SPAN, weights.shape[1]), lambda c: (c, 0)),
        ],
        out_specs=[
            pl.BlockSpec((SPAN, out_width), lambda c: (c, 0)),
            pl.BlockSpec((SPAN, out_width), lambda c: (c, 0)),
            pl.BlockSpec((heads, head_size, head_size), lambda c: (0, 0, 0)),
        ],
        out_shape=[
            jax.ShapeDtypeStruct((length, out_width), jnp.bfloat16),
            jax.ShapeDtypeStruct((length, out_width), jnp.float32),
            jax.ShapeDtypeStruct((heads, head_size, head_size), jnp.float32),
        ],
        scratch_shapes=[
            pltpu.VMEM((SPAN, model_width), jnp.bfloat16),
            pltpu.VMEM((SPAN, width), jnp.bfloat16),
        ],
        compiler_params=pltpu.CompilerParams(vmem_limit_bytes=VMEM_LIMIT),
        cost_estimate=pl.CostEstimate(
            flops=2 * length * model_width * width + 2 * length * out_width * SPAN,
            bytes_accessed=2 * length * model_width + 2 * model_width * width + 6 * length * out_width,
            transcendentals=0,
        ),
        name="near",
    )(rows, gain, projection, weights)


def far_kernel(heads, head_size, level_count, first_level, seq, held, *refs):
    scalar_ref, q_ref, near_ref, weight_ref = refs[:4]
    sibling_refs = refs[4 : 4 + level_count]
    out_ref = refs[-1]
    own = scalar_ref[0]
    rows = q_ref.shape[0]
    start = own * (rows * pl.num_programs(0)) + pl.program_id(0) * rows
    valid = start + lax.broadcasted_iota(jnp.int32, (rows, 1), 0) < scalar_ref[1 + seq]
    for h in range(heads):
        cols = slice(h * head_size, (h + 1) * head_size)
        q = q_ref[:, cols]
        acc = near_ref[:, cols]
        for j in range(level_count):
            upper = ((own >> j) & 1) == 1
            bucket = jnp.where(upper, sibling_refs[j][h], 0.0).astype(jnp.bfloat16)
            at = h * STRIDE + first_level + j
            acc = acc + weight_ref[:, at : at + 1] * dot32(q, bucket)
        acc = acc * lax.rsqrt(jnp.mean(acc * acc, -1, keepdims=True) + 1e-06)
        out_ref[0, :, cols] = jnp.where(valid, acc, 0.0).astype(jnp.bfloat16)


def far_call(seq, batch, held, scalars, q, near, weights, siblings, first_level, heads, head_size):
    length, out_width = q.shape
    tile = min(SPAN, length)
    spec = pl.BlockSpec((tile, out_width), lambda c: (c, 0))
    in_specs = [
        pl.BlockSpec(memory_space=pltpu.SMEM),
        spec,
        spec,
        pl.BlockSpec((tile, weights.shape[1]), lambda c: (c, 0)),
    ] + [pl.BlockSpec((heads, head_size, head_size), lambda c: (0, 0, 0)) for _ in siblings]
    operands = [scalars, q, near, weights, *siblings]
    aliases = {}
    if held is not None:
        aliases = {len(operands): 0}
        operands.append(held)
        in_specs.append(pl.BlockSpec(memory_space=pl.ANY))
    return pl.pallas_call(
        functools.partial(
            far_kernel, heads, head_size, len(siblings), first_level, seq, held is not None
        ),
        grid=(length // tile,),
        in_specs=in_specs,
        out_specs=pl.BlockSpec((1, tile, out_width), lambda c: (seq, c, 0)),
        out_shape=jax.ShapeDtypeStruct((batch, length, out_width), jnp.bfloat16),
        input_output_aliases=aliases,
        compiler_params=pltpu.CompilerParams(vmem_limit_bytes=VMEM_LIMIT),
        cost_estimate=pl.CostEstimate(
            flops=2 * length * out_width * head_size * len(siblings),
            bytes_accessed=8 * length * out_width,
            transcendentals=0,
        ),
        name="far",
    )(*operands)


def on_device(tokens, norm_gain, projection, level_table, level_index, lengths):
    batch_seqs, row_count, model_width = tokens.shape
    table_count, heads, level_total = level_table.shape
    head_size = projection.shape[1] // (3 * heads)
    block_len = row_count * lax.axis_size("head")
    span_count = block_len // SPAN
    local_bits = span_count.bit_length() - 1
    lchunk = SPAN.bit_length() - 1
    seq_bits = lax.axis_size("seq").bit_length() - 1
    own_index = lax.axis_index("seq")

    gathered = [
        lax.all_gather(tokens[s], "head", axis=0, tiled=True) for s in range(batch_seqs)
    ]
    table = jnp.pad(level_table, ((0, 0), (0, 0), (0, STRIDE - level_total)))
    table = table.reshape(table_count, heads * STRIDE)
    onehot = (level_index[..., None] == jnp.arange(table_count, dtype=jnp.int32)).astype(
        jnp.float32
    )
    weights = [
        jnp.dot(onehot[s], table, precision=lax.Precision.HIGHEST) for s in range(batch_seqs)
    ]
    scalars = jnp.concatenate([own_index.astype(jnp.int32)[None], lengths])
    gain = norm_gain[None]

    attended = None
    for s in range(batch_seqs):
        q, near, total = near_call(gathered[s], gain, projection, weights[s], heads, head_size)
        siblings = []
        block_sum = total
        for bit in range(seq_bits):
            sibling = swapped(block_sum, "seq", bit)
            siblings.append(sibling)
            block_sum = block_sum + sibling
        attended = far_call(
            s, batch_seqs, attended, scalars, q, near, weights[s], siblings,
            lchunk + local_bits + 1, heads, head_size,
        )
    return attended


def solution(mesh):
    in_specs = (
        P(None, ("seq", "head"), None),
        P(),
        P(None, "head"),
        P(None, "head", None),
        P(None, "seq"),
        P(),
    )
    out_specs = P(None, "seq", "head")
    return jax.shard_map(
        on_device, mesh=mesh, in_specs=in_specs, out_specs=out_specs, check_vma=False
    )
```

time: 297 us -> 231 us (0.78)
  matrix products: 53.9 us -> 2.33 us
  Pallas kernels: 0 us -> 51.4 us
  local copies, waits for them, and re-layouts: 49.4 us -> 4.67 us
  other arithmetic: 16.7 us -> 2.1 us
  waiting for transfers between devices: 159 us -> 150 us
  starting transfers between devices: 3.12 us -> 6.44 us
    dot_general x10 -> x2, matrix products: 53.9 us -> 2.33 us  [on_device(): jnp.dot(onehot[s], table, precision=lax.Precision.HIGHEST)]
    pallas_call x0 -> x4, Pallas kernels: none -> 51.4 us  [the longest x2 40 us: near_call(): pl.pallas_call(functools.partial(near_kernel, heads, head_size), grid=(le...]
    convert_element_type x8 -> x0, other arithmetic: 12.8 us -> none  [the longest x5 5.9 us: on_device(): (level_grid == level_step).astype(jnp.float32)]
    another operation x1 -> x0, local copies, waits for them, and re-layouts: 11.1 us -> none  [on_device(): projected_here.reshape(batch_seqs, span_count, SPAN, heads_here, 3, head_...]
    unnamed x20, local copies, waits for them, and re-layouts: 12.4 us -> 1.44 us
    convert_element_type x1 -> x0, local copies, waits for them, and re-layouts: 8.69 us -> none  [on_device(): projected_here.astype(jnp.bfloat16)]
    ppermute x3 -> x6, waiting for transfers between devices: 17 us -> 8.74 us  [swapped(): lax.ppermute(array, axis, [(i, i ^ 1 << bit) for i in range(lax.axis_size...]
    slice x1, local copies, waits for them, and re-layouts: 7.6 us -> 3.14 us  [on_device(): tokens[s]]
  transfers between devices with their start and end apart: 4 -> 8, of which waited for: 3 -> 6; matrix products, arithmetic and copies ran while one was open for 15% -> 2% of each run, Pallas kernels for 0% -> 20%
where the time goes in v1:
time: 231 us
  waiting for transfers between devices  150 us (65%)
  Pallas kernels  51.4 us (22%)
  between operations  13.5 us (6%)
  starting transfers between devices  6.44 us (3%)
  local copies, waits for them, and re-layouts  4.67 us (2%)
  matrix products  2.33 us (1%)
    all_gather x2, waiting for transfers between devices, on_device(): lax.all_gather(tokens[s], 'head', axis=0, tiled=True)  141 us
    pallas_call x2, Pallas kernels, near_call(): pl.pallas_call(functools.partial(near_kernel, heads, head_size), grid=(le...  40 us
    pallas_call x2, Pallas kernels, far_call(): pl.pallas_call(functools.partial(far_kernel, heads, head_size, len(siblin...  11.4 us
    ppermute x6, waiting for transfers between devices, swapped(): lax.ppermute(array, axis, [(i, i ^ 1 << bit) for i in range(lax.axis_size...  8.74 us
    ppermute x6, starting transfers between devices, swapped(): lax.ppermute(array, axis, [(i, i ^ 1 << bit) for i in range(lax.axis_size...  6.4 us
  transfers between devices with their start and end apart: 8, of which 6 were waited for; matrix products, arithmetic and copies ran while one was open for 2% of the time, Pallas kernels for 20%

profile of v1, /device:TPU:0, one launch (start us, length us, event | category | flops | bytes accessed | tf_op | source)
XLA Modules:
  0.0 230.9 jit_solution(13035544766306111)
XLA Ops:
  6.5 0.0 all-gather.7.cloned.1.call-start
  6.5 3.1 %fusion.2 = (bf16[1,256,2048]{2,1,0:T(8,128)(2,1)}, bf16[1,256,2048]{2,1,0:T(8,128)(2,1)}) fusion(bf16[2,256,2048]{2,1,0:T(8,128)(2,1)} %param.6), kind=kLoop, calls=%fused_computation.6 | loop fusion | bytes 4194304 | tf_op jit(solution)/shard_map/slice | solution.py:193
  9.7 0.0 copy-start.8
  9.7 0.0 all-gather.7.cloned.1.call-update
  9.7 0.0 all-gather.5.cloned.1.call-start
  9.8 0.7 all-gather.5.cloned.1.call-update
  10.5 0.0 copy-done.7
  10.5 0.1 reshape.4
  10.6 0.0 copy-done.8
  10.6 0.3 iota_compare_fusion
  10.9 1.1 fusion.weight_ref.refs_3_
  12.1 1.2 fusion.1.weight_ref.refs_3_
  13.3 80.1 %all-gather.7.cloned.1.call-done = bf16[1,1024,2048]{2,1,0:T(8,128)(2,1)} async-done(((bf16[1,256,2048]{2,1,0:T(8,128)(2,1)}), bf16[1,1024,2048]{2,1,0:T(8,128)(2,1)}) %all-gather.7.cloned.1.call-update) | async-done | bytes 4194320 | tf_op jit(solution)/shard_map/all_gather | solution.py:193
  93.3 20.0 %near.3 = (bf16[1024,512]{1,0:T(8,128)(2,1)}, f32[1024,512]{1,0:T(8,128)}, f32[4,128,128]{2,1,0:T(8,128)}) custom-call(bf16[1024,2048]{1,0:T(8,128)(2,1)} %bitcast.13, f32[1,2048]{1,0:T(1,128)} %bitcast.14, bf16[2048,1536]{1,0:T(8,128)(2,1)} %proj_ref.3, f32[1024,128]{1,0:T(8,128)} %fusion.weight_ref.refs_3_), custom_call_target="tpu_custom_call" | custom-call | flops 6979321856 | bytes 13631488 | tf_op jit(solution)/shard_map/near/pallas_call | solution.py:92
  113.3 0.1 collective-permute-start.3
  113.4 60.8 %all-gather.5.cloned.1.call-done = bf16[1,1024,2048]{2,1,0:T(8,128)(2,1)} async-done(((bf16[1,256,2048]{2,1,0:T(8,128)(2,1)}), bf16[1,1024,2048]{2,1,0:T(8,128)(2,1)}) %all-gather.5.cloned.1.call-update) | async-done | bytes 4194320 | tf_op jit(solution)/shard_map/all_gather | solution.py:193
  174.2 0.0 copy-start.5
  174.2 20.0 %near.2 = (bf16[1024,512]{1,0:T(8,128)(2,1)}, f32[1024,512]{1,0:T(8,128)}, f32[4,128,128]{2,1,0:T(8,128)}) custom-call(bf16[1024,2048]{1,0:T(8,128)(2,1)} %bitcast.12, f32[1,2048]{1,0:T(1,128)} %bitcast.15, bf16[2048,1536]{1,0:T(8,128)(2,1)} %proj_ref.3, f32[1024,128]{1,0:T(8,128)} %fusion.1.weight_ref.refs_3_), custom_call_target="tpu_custom_call" | custom-call | flops 6979321856 | bytes 13631488 | tf_op jit(solution)/shard_map/near/pallas_call | solution.py:92
  194.3 0.0 copy-start.9
  194.3 0.1 collective-permute-start
  194.4 0.0 collective-permute-done.3.refs_4_
  194.4 0.0 copy-done.5
  194.4 0.0 copy-start.2
  194.4 1.6 collective-permute-start.4
  196.0 0.1 collective-permute-done.refs_4_
  196.1 0.0 copy-start
  196.1 1.1 add.14
  197.2 1.6 collective-permute-start.1
  198.7 4.9 %collective-permute-done.4.refs_5_ = f32[4,128,128]{2,1,0:T(8,128)S(1)} collective-permute-done((f32[4,128,128]{2,1,0:T(8,128)S(1)}, f32[4,128,128]{2,1,0:T(8,128)S(1)}, u32[]{:S(2)}, u32[]{:S(2)}) %collective-permute-start.4) | collective-permute-done | bytes 262176 | tf_op jit(solution)/shard_map/ppermute | solution.py:19
  203.6 0.0 copy-start.3
  203.6 1.6 collective-permute-start.5
  205.2 3.6 %collective-permute-done.1.refs_5_ = f32[4,128,128]{2,1,0:T(8,128)S(1)} collective-permute-done((f32[4,128,128]{2,1,0:T(8,128)S(1)}, f32[4,128,128]{2,1,0:T(8,128)S(1)}, u32[]{:S(2)}, u32[]{:S(2)}) %collective-permute-start.1) | collective-permute-done | bytes 262176 | tf_op jit(solution)/shard_map/ppermute | solution.py:19
  208.8 0.0 copy-start.1
  208.8 1.6 collective-permute-start.2
  210.4 0.0 copy-done.9
  210.4 0.6 pad_add_fusion.refs_0_
  211.0 0.2 collective-permute-done.5.refs_6_
  211.2 0.0 copy-start.6
  211.2 0.0 copy-done.2
  211.2 0.0 copy-done.3
  211.2 0.7 copy-done.6
  211.9 5.7 %far.2.refs_7_ = bf16[2,1024,512]{2,1,0:T(8,128)(2,1)} custom-call(s32[3]{0:T(128)} %pad_add_fusion.refs_0_, bf16[1024,512]{1,0:T(8,128)(2,1)} %get-tuple-element.14.refs_1_, f32[1024,512]{1,0:T(8,128)} %get-tuple-element.15.refs_2_, f32[1024,128]{1,0:T(8,128)} %fusion.weight_ref.refs_3_, f32[4,128,128]{2,1,0:T(8,128)} %copy-done.2, ...), custom_call_target="tpu_custom_call" | custom-call | flops 402653184 | bytes 4194304 | tf_op jit(solution)/shard_map/far/pallas_call | solution.py:162
  217.6 0.0 copy-done
  217.6 0.0 copy-done.1
  217.6 0.0 collective-permute-done.2.refs_6_
  217.6 0.0 copy-start.4
  217.6 0.7 copy-done.4
  218.3 5.7 %far.3 = bf16[2,1024,512]{2,1,0:T(8,128)(2,1)} custom-call(s32[3]{0:T(128)} %pad_add_fusion.refs_0_, bf16[1024,512]{1,0:T(8,128)(2,1)} %get-tuple-element.11.refs_1_, f32[1024,512]{1,0:T(8,128)} %get-tuple-element.12.refs_2_, f32[1024,128]{1,0:T(8,128)} %fusion.1.weight_ref.refs_3_, f32[4,128,128]{2,1,0:T(8,128)} %copy-done, ...), custom_call_target="tpu_custom_call", output_to_operand_aliasing={{}: (7, {})} | custom-call | flops 402653184 | bytes 4194304 | tf_op jit(solution)/shard_map/far/pallas_call | solution.py:162
  (5 shorter events, 0.1 us)
Async XLA Ops:
  6.5 86.8 %all-gather.7.cloned.1.call-start = ((), (), s32[]{:S(2)}) async-start(), calls=%async_computation.1 | async-start | bytes 5242880 | tf_op jit(solution)/shard_map/all_gather | solution.py:193
  9.7 0.8 copy-start.7
  9.7 0.9 copy-start.8
  9.7 164.5 %all-gather.5.cloned.1.call-start = ((), (), s32[]{:S(2)}) async-start(), calls=%async_computation | async-start | bytes 5242880 | tf_op jit(solution)/shard_map/all_gather | solution.py:193
  113.3 81.0 %collective-permute-start.3 = (f32[4,128,128]{2,1,0:T(8,128)}, f32[4,128,128]{2,1,0:T(8,128)S(1)}, u32[]{:S(2)}, u32[]{:S(2)}) collective-permute-start(f32[4,128,128]{2,1,0:T(8,128)} %get-tuple-element.16), channel_id=1, source_target_pairs={{0,4},{4,0},{8,12},{12,8},{16,20},{20,16},{24,28},{28,24},{1,5},{5... | collective-permute-start | bytes 786440 | tf_op jit(solution)/shard_map/ppermute | solution.py:19
  174.2 20.1 %copy-start.5 = (f32[4,128,128]{2,1,0:T(8,128)S(1)}, f32[4,128,128]{2,1,0:T(8,128)}, u32[]{:S(2)}) copy-start(f32[4,128,128]{2,1,0:T(8,128)} %get-tuple-element.16) | copy-start | bytes 786436
  194.3 16.1 %copy-start.9 = (s32[2]{0:T(128)S(1)}, s32[2]{0:T(128)}, u32[]{:S(2)}) copy-start(s32[2]{0:T(128)} %param.11) | copy-start | bytes 28
  194.3 1.8 collective-permute-start
  194.4 16.8 %copy-start.2 = (f32[4,128,128]{2,1,0:T(8,128)}, f32[4,128,128]{2,1,0:T(8,128)S(1)}, u32[]{:S(2)}) copy-start(f32[4,128,128]{2,1,0:T(8,128)S(1)} %collective-permute-done.3.refs_4_) | copy-start | bytes 786436
  194.4 9.2 %collective-permute-start.4 = (f32[4,128,128]{2,1,0:T(8,128)S(1)}, f32[4,128,128]{2,1,0:T(8,128)S(1)}, u32[]{:S(2)}, u32[]{:S(2)}) collective-permute-start(f32[4,128,128]{2,1,0:T(8,128)S(1)} %add.16), channel_id=1, source_target_pairs={{0,8},{4,12},{8,0},{12,4},{16,24},{20,28},{24,16},{28,20},{1,9},{5... | collective-permute-start | bytes 786440 | tf_op jit(solution)/shard_map/ppermute | solution.py:19
  196.1 21.5 %copy-start = (f32[4,128,128]{2,1,0:T(8,128)}, f32[4,128,128]{2,1,0:T(8,128)S(1)}, u32[]{:S(2)}) copy-start(f32[4,128,128]{2,1,0:T(8,128)S(1)} %collective-permute-done.refs_4_) | copy-start | bytes 786436
  197.2 11.6 %collective-permute-start.1 = (f32[4,128,128]{2,1,0:T(8,128)S(1)}, f32[4,128,128]{2,1,0:T(8,128)S(1)}, u32[]{:S(2)}, u32[]{:S(2)}) collective-permute-start(f32[4,128,128]{2,1,0:T(8,128)S(1)} %add.14), channel_id=1, source_target_pairs={{0,8},{4,12},{8,0},{12,4},{16,24},{20,28},{24,16},{28,20},{1,9},{5... | collective-permute-start | bytes 786440 | tf_op jit(solution)/shard_map/ppermute | solution.py:19
  203.6 7.6 %copy-start.3 = (f32[4,128,128]{2,1,0:T(8,128)}, f32[4,128,128]{2,1,0:T(8,128)S(1)}, u32[]{:S(2)}) copy-start(f32[4,128,128]{2,1,0:T(8,128)S(1)} %collective-permute-done.4.refs_5_) | copy-start | bytes 786436
  203.6 7.5 %collective-permute-start.5 = (f32[4,128,128]{2,1,0:T(8,128)S(1)}, f32[4,128,128]{2,1,0:T(8,128)S(1)}, u32[]{:S(2)}, u32[]{:S(2)}) collective-permute-start(f32[4,128,128]{2,1,0:T(8,128)S(1)} %add.17), channel_id=1, source_target_pairs={{0,16},{4,20},{8,24},{12,28},{16,0},{20,4},{24,8},{28,12},{1,17},{... | collective-permute-start | bytes 786440 | tf_op jit(solution)/shard_map/ppermute | solution.py:19
  208.8 8.8 %copy-start.1 = (f32[4,128,128]{2,1,0:T(8,128)}, f32[4,128,128]{2,1,0:T(8,128)S(1)}, u32[]{:S(2)}) copy-start(f32[4,128,128]{2,1,0:T(8,128)S(1)} %collective-permute-done.1.refs_5_) | copy-start | bytes 786436
  208.8 8.8 %collective-permute-start.2 = (f32[4,128,128]{2,1,0:T(8,128)S(1)}, f32[4,128,128]{2,1,0:T(8,128)S(1)}, u32[]{:S(2)}, u32[]{:S(2)}) collective-permute-start(f32[4,128,128]{2,1,0:T(8,128)S(1)} %add.15), channel_id=1, source_target_pairs={{0,16},{4,20},{8,24},{12,28},{16,0},{20,4},{24,8},{28,12},{1,17},{... | collective-permute-start | bytes 786440 | tf_op jit(solution)/shard_map/ppermute | solution.py:19
  211.2 0.7 copy-start.6
  217.6 0.7 copy-start.4
Sparse Core Ops, SparseCore 0:
  9.8 83.4 all-gather.6
  94.9 79.2 all-gather.4

commit v2 on v0

v2 whole, which is shorter than its diff:
```python
import functools

import jax
import jax.numpy as jnp
from jax import lax
from jax.experimental import pallas as pl
from jax.experimental.pallas import tpu as pltpu
from jax.sharding import PartitionSpec as P

SPAN = 512
LANE = 128
STRIDE = 32
VMEM_LIMIT = 56 * 1024 * 1024
NT = (((1,), (1,)), ((), ()))
TN = (((0,), (0,)), ((), ()))
MESH = pl.DeviceIdType.MESH


def dot32(a, b):
    return jnp.dot(a, b, preferred_element_type=jnp.float32)


def kernel(
    dims,
    tokens_ref, gain_ref, proj_hbm, table_ref, index_ref, lengths_ref,
    out_ref,
    rows_buf, proj_ref, normed, qkv, near, weights, total, outbox, inbox,
    own_sem, proj_sem, send_sem, recv_sem, tree_send, tree_recv,
):
    heads, head_size, groups, seq_bits, span_count = dims
    batch, row_count, model_width = tokens_ref.shape
    block_len = row_count * groups
    width = proj_ref.shape[1]
    lchunk = SPAN.bit_length() - 1
    local_bits = span_count.bit_length() - 1
    first_level = lchunk + local_bits + 1
    me = lax.axis_index("head")
    own = lax.axis_index("seq")

    def flipped(bit):
        return own + (1 << bit) - 2 * (own & (1 << bit))

    proj_copy = pltpu.make_async_copy(proj_hbm, proj_ref, proj_sem)
    barrier = pltpu.get_barrier_semaphore()

    @pl.when(me > 0)
    def _():
        pl.semaphore_signal(barrier, inc=1, device_id={"head": me - 1}, device_id_type=MESH)

    @pl.when(me < groups - 1)
    def _():
        pl.semaphore_signal(barrier, inc=1, device_id={"head": me + 1}, device_id_type=MESH)

    for bit in range(seq_bits):
        pl.semaphore_signal(barrier, inc=1, device_id={"seq": flipped(bit)}, device_id_type=MESH)

    def own_copy(s):
        return pltpu.make_async_copy(tokens_ref.at[s], rows_buf.at[s, me], own_sem.at[s])

    for s in range(batch):
        own_copy(s).start()
    proj_copy.start()
    ends = (me == 0).astype(jnp.int32) + (me == groups - 1).astype(jnp.int32)
    pl.semaphore_wait(barrier, seq_bits + 2 - ends)

    def send_own(side, s):
        return pltpu.make_async_remote_copy(
            src_ref=tokens_ref.at[s], dst_ref=rows_buf.at[s, me],
            send_sem=send_sem.at[side, s, me], recv_sem=recv_sem.at[s, me],
            device_id={"head": me + 1 - 2 * side}, device_id_type=MESH,
        )

    def pass_on(side, s, owner):
        return pltpu.make_async_remote_copy(
            src_ref=rows_buf.at[s, owner], dst_ref=rows_buf.at[s, owner],
            send_sem=send_sem.at[side, s, owner], recv_sem=recv_sem.at[s, owner],
            device_id={"head": me + 1 - 2 * side}, device_id_type=MESH,
        )

    def has_next(side):
        return me < groups - 1 if side == 0 else me > 0

    for s in range(batch):
        for side in range(2):
            @pl.when(has_next(side))
            def _():
                send_own(side, s).start()

    proj_copy.wait()

    def project(s, owner):
        piece = 128
        for start in range(0, row_count, piece):
            x = rows_buf[s, owner, start : start + piece].astype(jnp.float32)
            scale = lax.rsqrt(jnp.mean(x * x, -1, keepdims=True) + 1e-06)
            normed[start : start + piece] = (x * scale * gain_ref[...]).astype(jnp.bfloat16)
        step = 2 * 3 * head_size if width % (6 * head_size) == 0 else 3 * head_size
        at = pl.ds(pl.multiple_of(owner * row_count, row_count), row_count)
        for col in range(0, width, step):
            qkv[s, at, col : col + step] = dot32(
                normed[...], proj_ref[:, col : col + step]
            ).astype(jnp.bfloat16)

    t = lax.broadcasted_iota(jnp.int32, (LANE, LANE), 0)
    u = lax.broadcasted_iota(jnp.int32, (LANE, LANE), 1)
    apart = t ^ u
    level = jnp.zeros((LANE, LANE), jnp.int32)
    for shift in range(LANE.bit_length() - 1):
        level = level + (apart >= 1 << shift).astype(jnp.int32)
    level = jnp.where(u <= t, level, STRIDE - 1)

    def near_span(s, span):
        base_row = span * SPAN
        at_span = pl.ds(pl.multiple_of(base_row, SPAN), SPAN)
        choice = index_ref[s, at_span, :]
        tables = lax.broadcasted_iota(jnp.int32, (SPAN, table_ref.shape[0]), 1)
        onehot = (choice == tables).astype(jnp.float32)
        weights[at_span, :] = jnp.dot(
            onehot, table_ref[...], precision=lax.Precision.HIGHEST,
            preferred_element_type=jnp.float32,
        )
        for h in range(heads):
            base = h * 3 * head_size
            q = qkv[s, at_span, base : base + head_size]
            k = qkv[s, at_span, base + head_size : base + 2 * head_size]
            v = qkv[s, at_span, base + 2 * head_size : base + 3 * head_size]
            out_cols = slice(h * head_size, (h + 1) * head_size)
            before = total[h]
            readout = dot32(q, before.astype(jnp.bfloat16))
            for start in range(0, SPAN, LANE):
                rows = slice(start, start + LANE)
                at_rows = pl.ds(pl.multiple_of(base_row + start, LANE), LANE)
                w_rows = weights[at_rows, :]
                grid = jnp.take_along_axis(w_rows, level + h * STRIDE, axis=1)
                scores = lax.dot_general(q[rows], k[rows], NT, preferred_element_type=jnp.float32)
                acc = dot32((scores * grid).astype(jnp.bfloat16), v[rows])
                far_at = h * STRIDE + lchunk + 1
                acc = acc + w_rows[:, far_at : far_at + 1] * readout[rows]
                size = LANE
                while size < SPAN:
                    if start & size:
                        low = start & ~(2 * size - 1)
                        at = h * STRIDE + size.bit_length()
                        scores = lax.dot_general(
                            q[rows], k[low : low + size], NT, preferred_element_type=jnp.float32
                        )
                        scores = (scores * w_rows[:, at : at + 1]).astype(jnp.bfloat16)
                        acc = acc + dot32(scores, v[low : low + size])
                    size *= 2
                near[at_rows, out_cols] = acc
            total[h] = before + lax.dot_general(k, v, TN, preferred_element_type=jnp.float32)

    def exchange(s, bit):
        return pltpu.make_async_remote_copy(
            src_ref=outbox.at[s, bit], dst_ref=inbox.at[s, bit],
            send_sem=tree_send.at[s, bit], recv_sem=tree_recv.at[s, bit],
            device_id={"seq": flipped(bit)}, device_id_type=MESH,
        )

    def far_span(s, span):
        base_row = span * SPAN
        at_span = pl.ds(pl.multiple_of(base_row, SPAN), SPAN)
        first = own * block_len + base_row
        valid = first + lax.broadcasted_iota(jnp.int32, (SPAN, 1), 0) < lengths_ref[s]
        w_rows = weights[at_span, :]
        for h in range(heads):
            cols = slice(h * head_size, (h + 1) * head_size)
            base = h * 3 * head_size
            q = qkv[s, at_span, base : base + head_size]
            acc = near[at_span, cols]
            for j in range(seq_bits):
                upper = ((own >> j) & 1) == 1
                bucket = jnp.where(upper, inbox[s, j, h].astype(jnp.float32), 0.0)
                at = h * STRIDE + first_level + j
                acc = acc + w_rows[:, at : at + 1] * dot32(q, bucket.astype(jnp.bfloat16))
            acc = acc * lax.rsqrt(jnp.mean(acc * acc, -1, keepdims=True) + 1e-06)
            out_ref[s, at_span, cols] = jnp.where(valid, acc, 0.0).astype(jnp.bfloat16)

    def finish(s):
        total[...] = jnp.zeros_like(total)

        @pl.loop(0, span_count)
        def _(span):
            near_span(s, span)

        for bit in range(seq_bits):
            outbox[s, bit] = total[...].astype(jnp.bfloat16)
            exchange(s, bit).start()
            exchange(s, bit).wait_recv()
            if bit < seq_bits - 1:
                total[...] = total[...] + inbox[s, bit].astype(jnp.float32)

        @pl.loop(0, span_count)
        def _(span):
            far_span(s, span)

    @pl.loop(0, batch)
    def _(s):
        own_copy(s).wait()
        project(s, me)

    @pl.loop(0, (groups - 1) * batch)
    def _(event):
        d = event // batch + 1
        s = event % batch
        for side in range(2):
            owner = me - d if side == 0 else me + d
            present = owner >= 0 if side == 0 else owner < groups

            @pl.when(present)
            def _():
                pass_on(side, s, owner).wait_recv()

                @pl.when(has_next(side))
                def _():
                    pass_on(side, s, owner).start()

        @pl.loop(0, 2)
        def _(way):
            owner = me - d + 2 * d * way

            @pl.when((owner >= 0) & (owner < groups))
            def _():
                project(s, owner)

        @pl.when(d == groups - 1)
        def _():
            finish(s)

    for s in range(batch):
        for side in range(2):
            @pl.when(has_next(side))
            def _():
                send_own(side, s).wait_send()

                for d in range(1, groups - 1):
                    owner = me - d if side == 0 else me + d

                    @pl.when(owner >= 0 if side == 0 else owner < groups)
                    def _():
                        pass_on(side, s, owner).wait_send()

        for bit in range(seq_bits):
            exchange(s, bit).wait_send()


def on_device(tokens, norm_gain, projection, level_table, level_index, lengths):
    batch, row_count, model_width = tokens.shape
    table_count, heads, level_total = level_table.shape
    width = projection.shape[1]
    head_size = width // (3 * heads)
    groups = lax.axis_size("head")
    block_len = row_count * groups
    span_count = block_len // SPAN
    seq_bits = lax.axis_size("seq").bit_length() - 1
    table = jnp.pad(level_table, ((0, 0), (0, 0), (0, STRIDE - level_total)))
    table = table.reshape(table_count, heads * STRIDE)
    out_width = heads * head_size
    vmem = pl.BlockSpec(memory_space=pltpu.VMEM)
    hbm = pl.BlockSpec(memory_space=pl.ANY)
    states = (batch, seq_bits, heads, head_size, head_size)
    return pl.pallas_call(
        functools.partial(kernel, (heads, head_size, groups, seq_bits, span_count)),
        in_specs=[hbm, vmem, hbm, vmem, vmem, pl.BlockSpec(memory_space=pltpu.SMEM)],
        out_specs=vmem,
        out_shape=jax.ShapeDtypeStruct((batch, block_len, out_width), jnp.bfloat16),
        scratch_shapes=[
            pltpu.VMEM((batch, groups, row_count, model_width), jnp.bfloat16),
            pltpu.VMEM((model_width, width), jnp.bfloat16),
            pltpu.VMEM((row_count, model_width), jnp.bfloat16),
            pltpu.VMEM((batch, block_len, width), jnp.bfloat16),
            pltpu.VMEM((block_len, out_width), jnp.float32),
            pltpu.VMEM((block_len, heads * STRIDE), jnp.float32),
            pltpu.VMEM((heads, head_size, head_size), jnp.float32),
            pltpu.VMEM(states, jnp.bfloat16),
            pltpu.VMEM(states, jnp.bfloat16),
            pltpu.SemaphoreType.DMA((batch,)),
            pltpu.SemaphoreType.DMA,
            pltpu.SemaphoreType.DMA((2, batch, groups)),
            pltpu.SemaphoreType.DMA((batch, groups)),
            pltpu.SemaphoreType.DMA((batch, seq_bits)),
            pltpu.SemaphoreType.DMA((batch, seq_bits)),
        ],
        compiler_params=pltpu.CompilerParams(
            vmem_limit_bytes=VMEM_LIMIT, collective_id=0, has_side_effects=True
        ),
        name="attend",
    )(tokens, norm_gain[None], projection, table, level_index[..., None], lengths)


def solution(mesh):
    in_specs = (
        P(None, ("seq", "head"), None),
        P(),
        P(None, "head"),
        P(None, "head", None),
        P(None, "seq"),
        P(),
    )
    out_specs = P(None, "seq", "head")
    return jax.shard_map(
        on_device, mesh=mesh, in_specs=in_specs, out_specs=out_specs, check_vma=False
    )
```

time: 297 us -> 177 us (0.60)
  Pallas kernels: 0 us -> 170 us
  waiting for transfers between devices: 159 us -> 0 us
  matrix products: 53.9 us -> 0 us
  local copies, waits for them, and re-layouts: 49.4 us -> 6.52 us
  other arithmetic: 16.7 us -> 0 us
  between operations: 13.8 us -> 0.01 us
  starting transfers between devices: 3.12 us -> 0 us
    pallas_call x0 -> x1, Pallas kernels: none -> 170 us  [on_device(): pl.pallas_call(functools.partial(kernel, (heads, head_size, groups, seq_b...]
    all_gather x1 -> x0, waiting for transfers between devices: 142 us -> none  [on_device(): block_rows = lax.all_gather(normed, 'head', axis=1, tiled=True)]
    dot_general x10 -> x0, matrix products: 53.9 us -> none  [the longest x1 20.1 us: on_device(): jnp.einsum('scthd,scuhd->schtu', queries, keys_here, preferred_element_ty...]
    ppermute x3 -> x0, waiting for transfers between devices: 17 us -> none  [swapped(): lax.ppermute(array, axis, [(i, i ^ 1 << bit) for i in range(lax.axis_size...]
    convert_element_type x8 -> x0, other arithmetic: 12.8 us -> none  [the longest x5 5.9 us: on_device(): (level_grid == level_step).astype(jnp.float32)]
    another operation x1 -> x0, local copies, waits for them, and re-layouts: 11.1 us -> none  [on_device(): projected_here.reshape(batch_seqs, span_count, SPAN, heads_here, 3, head_...]
    unnamed x20 -> x1, local copies, waits for them, and re-layouts: 12.4 us -> 3.05 us
    convert_element_type x1 -> x0, local copies, waits for them, and re-layouts: 8.69 us -> none  [on_device(): projected_here.astype(jnp.bfloat16)]
  transfers between devices with their start and end apart: 4 -> 0, of which waited for: 3 -> 0; matrix products, arithmetic and copies ran while one was open for 15% -> 0% of each run, Pallas kernels for 0% -> 0%
where the time goes in v2:
time: 177 us
  Pallas kernels  170 us (96%)
  local copies, waits for them, and re-layouts  6.52 us (4%)
    pallas_call x1, Pallas kernels, on_device(): pl.pallas_call(functools.partial(kernel, (heads, head_size, groups, seq_b...  170 us

profile of v2, /device:TPU:0, one launch (start us, length us, event | category | flops | bytes accessed | tf_op | source)
XLA Modules:
  0.0 176.9 jit_solution(4038210130474969361)
XLA Ops:
  0.0 0.8 pad.4
  0.8 0.7 reshape.3.table_ref
  1.4 2.0 %copy.7.index_ref = s32[2,1024,1]{2,1,0:T(8,128)} copy(s32[2,1024,1]{1,0,2:T(2,128)} %bitcast.2) | data formatting | bytes 16384 | tf_op jit(solution)/shard_map/broadcast_in_dim | solution.py:288
  3.5 170.3 %attend.1 = bf16[2,1024,512]{2,1,0:T(8,128)(2,1)} custom-call(bf16[2,256,2048]{2,1,0:T(8,128)(2,1)} %tokens_ref.1, f32[1,2048]{1,0:T(1,128)} %bitcast.3, bf16[2048,1536]{1,0:T(8,128)(2,1)} %proj_hbm.1, f32[16,128]{1,0:T(8,128)} %reshape.3.table_ref, s32[2,1024,1]{2,1,0:T(8,128)} %copy.7.index_ref, s32[2]{0:T(128)} %lengths_ref.1), custom_call_target="tpu_custom_call" | custom-call | tf_op jit(solution)/shard_map/attend/pallas_call | solution.py:262
  173.8 3.0 %copy.9 = bf16[2,1024,512]{2,1,0:T(8,128)(2,1)} copy(bf16[2,1024,512]{2,1,0:T(8,128)(2,1)} %attend.1) | data formatting | bytes 4194304

commit v3 on v2

--- a/solution.py
+++ b/solution.py
@@ -24,7 +24,7 @@
     dims,
     tokens_ref, gain_ref, proj_hbm, table_ref, index_ref, lengths_ref,
     out_ref,
-    rows_buf, proj_ref, normed, qkv, near, weights, total, outbox, inbox,
+    rows_buf, proj_ref, normed, qkv, near, weights, states, total, outbox, inbox,
     own_sem, proj_sem, send_sem, recv_sem, tree_send, tree_recv,
 ):
     heads, head_size, groups, seq_bits, span_count = dims
@@ -33,6 +33,7 @@
     width = proj_ref.shape[1]
     lchunk = SPAN.bit_length() - 1
     local_bits = span_count.bit_length() - 1
+    shards = SPAN // row_count
     first_level = lchunk + local_bits + 1
     me = lax.axis_index("head")
     own = lax.axis_index("seq")
@@ -85,8 +86,6 @@
             @pl.when(has_next(side))
             def _():
                 send_own(side, s).start()
-
-    proj_copy.wait()
 
     def project(s, owner):
         piece = 128
@@ -109,46 +108,52 @@
         level = level + (apart >= 1 << shift).astype(jnp.int32)
     level = jnp.where(u <= t, level, STRIDE - 1)
 
-    def near_span(s, span):
+    for s in range(batch):
+        for start in range(0, block_len, SPAN):
+            tables = lax.broadcasted_iota(jnp.int32, (table_ref.shape[0], SPAN), 0)
+            onehot = (index_ref[s : s + 1, start : start + SPAN] == tables).astype(jnp.float32)
+            weights[s, start : start + SPAN, :] = lax.dot_general(
+                onehot, table_ref[...], TN, precision=lax.Precision.HIGHEST,
+                preferred_element_type=jnp.float32,
+            )
+
+    proj_copy.wait()
+
+    def span_states(s, span):
+        at_span = pl.ds(pl.multiple_of(span * SPAN, SPAN), SPAN)
+        for h in range(heads):
+            base = h * 3 * head_size
+            k = qkv[s, at_span, base + head_size : base + 2 * head_size]
+            v = qkv[s, at_span, base + 2 * head_size : base + 3 * head_size]
+            states[s, span, h] = lax.dot_general(k, v, TN, preferred_element_type=jnp.float32)
+
+    def near_head(s, span, h):
         base_row = span * SPAN
         at_span = pl.ds(pl.multiple_of(base_row, SPAN), SPAN)
-        choice = index_ref[s, at_span, :]
-        tables = lax.broadcasted_iota(jnp.int32, (SPAN, table_ref.shape[0]), 1)
-        onehot = (choice == tables).astype(jnp.float32)
-        weights[at_span, :] = jnp.dot(
-            onehot, table_ref[...], precision=lax.Precision.HIGHEST,
-            preferred_element_type=jnp.float32,
-        )
-        for h in range(heads):
-            base = h * 3 * head_size
-            q = qkv[s, at_span, base : base + head_size]
-            k = qkv[s, at_span, base + head_size : base + 2 * head_size]
-            v = qkv[s, at_span, base + 2 * head_size : base + 3 * head_size]
-            out_cols = slice(h * head_size, (h + 1) * head_size)
-            before = total[h]
-            readout = dot32(q, before.astype(jnp.bfloat16))
-            for start in range(0, SPAN, LANE):
-                rows = slice(start, start + LANE)
-                at_rows = pl.ds(pl.multiple_of(base_row + start, LANE), LANE)
-                w_rows = weights[at_rows, :]
-                grid = jnp.take_along_axis(w_rows, level + h * STRIDE, axis=1)
-                scores = lax.dot_general(q[rows], k[rows], NT, preferred_element_type=jnp.float32)
-                acc = dot32((scores * grid).astype(jnp.bfloat16), v[rows])
-                far_at = h * STRIDE + lchunk + 1
-                acc = acc + w_rows[:, far_at : far_at + 1] * readout[rows]
-                size = LANE
-                while size < SPAN:
-                    if start & size:
-                        low = start & ~(2 * size - 1)
-                        at = h * STRIDE + size.bit_length()
-                        scores = lax.dot_general(
-                            q[rows], k[low : low + size], NT, preferred_element_type=jnp.float32
-                        )
-                        scores = (scores * w_rows[:, at : at + 1]).astype(jnp.bfloat16)
-                        acc = acc + dot32(scores, v[low : low + size])
-                    size *= 2
-                near[at_rows, out_cols] = acc
-            total[h] = before + lax.dot_general(k, v, TN, preferred_element_type=jnp.float32)
+        base = h * 3 * head_size
+        q = qkv[s, at_span, base : base + head_size]
+        k = qkv[s, at_span, base + head_size : base + 2 * head_size]
+        v = qkv[s, at_span, base + 2 * head_size : base + 3 * head_size]
+        out_cols = slice(h * head_size, (h + 1) * head_size)
+        for start in range(0, SPAN, LANE):
+            rows = slice(start, start + LANE)
+            at_rows = pl.ds(pl.multiple_of(base_row + start, LANE), LANE)
+            w_rows = weights[s, at_rows, :]
+            grid = jnp.take_along_axis(w_rows, level + h * STRIDE, axis=1)
+            scores = lax.dot_general(q[rows], k[rows], NT, preferred_element_type=jnp.float32)
+            acc = dot32((scores * grid).astype(jnp.bfloat16), v[rows])
+            size = LANE
+            while size < SPAN:
+                if start & size:
+                    low = start & ~(2 * size - 1)
+                    at = h * STRIDE + size.bit_length()
+                    scores = lax.dot_general(
+                        q[rows], k[low : low + size], NT, preferred_element_type=jnp.float32
+                    )
+                    scores = (scores * w_rows[:, at : at + 1]).astype(jnp.bfloat16)
+                    acc = acc + dot32(scores, v[low : low + size])
+                size *= 2
+            near[s, at_rows, out_cols] = acc
 
     def exchange(s, bit):
         return pltpu.make_async_remote_copy(
@@ -162,12 +167,16 @@
         at_span = pl.ds(pl.multiple_of(base_row, SPAN), SPAN)
         first = own * block_len + base_row
         valid = first + lax.broadcasted_iota(jnp.int32, (SPAN, 1), 0) < lengths_ref[s]
-        w_rows = weights[at_span, :]
+        w_rows = weights[s, at_span, :]
         for h in range(heads):
             cols = slice(h * head_size, (h + 1) * head_size)
             base = h * 3 * head_size
             q = qkv[s, at_span, base : base + head_size]
-            acc = near[at_span, cols]
+            acc = near[s, at_span, cols]
+            for j in range(span_count - 1):
+                earlier = jnp.where(span > j, states[s, j, h], 0.0).astype(jnp.bfloat16)
+                at = h * STRIDE + lchunk + 1
+                acc = acc + w_rows[:, at : at + 1] * dot32(q, earlier)
             for j in range(seq_bits):
                 upper = ((own >> j) & 1) == 1
                 bucket = jnp.where(upper, inbox[s, j, h].astype(jnp.float32), 0.0)
@@ -176,16 +185,27 @@
             acc = acc * lax.rsqrt(jnp.mean(acc * acc, -1, keepdims=True) + 1e-06)
             out_ref[s, at_span, cols] = jnp.where(valid, acc, 0.0).astype(jnp.bfloat16)
 
+    def last_shard(span):
+        low = span * shards
+        high = low + shards - 1
+        return jnp.maximum(jnp.maximum(me - low, low - me), jnp.maximum(me - high, high - me))
+
+    chunk = -(-heads // seq_bits)
+
     def finish(s):
-        total[...] = jnp.zeros_like(total)
-
-        @pl.loop(0, span_count)
-        def _(span):
-            near_span(s, span)
-
+        summed = states[s, 0]
+        for span in range(1, span_count):
+            summed = summed + states[s, span]
+        total[...] = summed
         for bit in range(seq_bits):
             outbox[s, bit] = total[...].astype(jnp.bfloat16)
             exchange(s, bit).start()
+            for h in range(bit * chunk, min(heads, (bit + 1) * chunk)):
+                @pl.loop(0, span_count)
+                def _(span):
+                    @pl.when(last_shard(span) == groups - 1)
+                    def _():
+                        near_head(s, span, h)
             exchange(s, bit).wait_recv()
             if bit < seq_bits - 1:
                 total[...] = total[...] + inbox[s, bit].astype(jnp.float32)
@@ -222,6 +242,17 @@
             @pl.when((owner >= 0) & (owner < groups))
             def _():
                 project(s, owner)
+
+        @pl.loop(0, span_count)
+        def _(span):
+            @pl.when(last_shard(span) == d)
+            def _():
+                span_states(s, span)
+
+                @pl.when(d < groups - 1)
+                def _():
+                    for h in range(heads):
+                        near_head(s, span, h)
 
         @pl.when(d == groups - 1)
         def _():
@@ -269,8 +300,9 @@
             pltpu.VMEM((model_width, width), jnp.bfloat16),
             pltpu.VMEM((row_count, model_width), jnp.bfloat16),
             pltpu.VMEM((batch, block_len, width), jnp.bfloat16),
-            pltpu.VMEM((block_len, out_width), jnp.float32),
-            pltpu.VMEM((block_len, heads * STRIDE), jnp.float32),
+            pltpu.VMEM((batch, block_len, out_width), jnp.float32),
+            pltpu.VMEM((batch, block_len, heads * STRIDE), jnp.float32),
+            pltpu.VMEM((batch, span_count, heads, head_size, head_size), jnp.float32),
             pltpu.VMEM((heads, head_size, head_size), jnp.float32),
             pltpu.VMEM(states, jnp.bfloat16),
             pltpu.VMEM(states, jnp.bfloat16),
@@ -285,7 +317,7 @@
             vmem_limit_bytes=VMEM_LIMIT, collective_id=0, has_side_effects=True
         ),
         name="attend",
-    )(tokens, norm_gain[None], projection, table, level_index[..., None], lengths)
+    )(tokens, norm_gain[None], projection, table, level_index, lengths)
 
 
 def solution(mesh):

time: 177 us -> 164 us (0.927)
  Pallas kernels: 170 us -> 160 us
  local copies, waits for them, and re-layouts: 6.52 us -> 4.49 us
    pallas_call x1, Pallas kernels: 170 us -> 160 us  [on_device(): pl.pallas_call(functools.partial(kernel, (heads, head_size, groups, seq_b...]
    broadcast_in_dim x1 -> x0, local copies, waits for them, and re-layouts: 2.04 us -> none  [on_device(): level_index[..., None]]
where the time goes in v3:
time: 164 us
  Pallas kernels  160 us (98%)
  local copies, waits for them, and re-layouts  4.49 us (3%)
    pallas_call x1, Pallas kernels, on_device(): pl.pallas_call(functools.partial(kernel, (heads, head_size, groups, seq_b...  160 us

profile of v3, /device:TPU:0, one launch (start us, length us, event | category | flops | bytes accessed | tf_op | source)
XLA Modules:
  0.0 164.0 jit_solution(8899363064264321343)
XLA Ops:
  0.0 0.8 pad.4
  0.8 0.7 reshape.3.table_ref
  1.4 159.5 %attend.1 = bf16[2,1024,512]{2,1,0:T(8,128)(2,1)} custom-call(bf16[2,256,2048]{2,1,0:T(8,128)(2,1)} %tokens_ref.1, f32[1,2048]{1,0:T(1,128)} %bitcast.1, bf16[2048,1536]{1,0:T(8,128)(2,1)} %proj_hbm.1, f32[16,128]{1,0:T(8,128)} %reshape.3.table_ref, s32[2,1024]{1,0:T(2,128)} %index_ref.1, s32[2]{0:T(128)} %lengths_ref.1), custom_call_target="tpu_custom_call" | custom-call | tf_op jit(solution)/shard_map/attend/pallas_call | solution.py:293
  161.0 3.0 %copy.8 = bf16[2,1024,512]{2,1,0:T(8,128)(2,1)} copy(bf16[2,1024,512]{2,1,0:T(8,128)(2,1)} %attend.1) | data formatting | bytes 4194304

commit v4 on v3

--- a/solution.py
+++ b/solution.py
@@ -162,11 +162,14 @@
             device_id={"seq": flipped(bit)}, device_id_type=MESH,
         )
 
-    def far_span(s, span):
-        base_row = span * SPAN
-        at_span = pl.ds(pl.multiple_of(base_row, SPAN), SPAN)
-        first = own * block_len + base_row
-        valid = first + lax.broadcasted_iota(jnp.int32, (SPAN, 1), 0) < lengths_ref[s]
+    def bucket_part(s, h, j, q, w_rows):
+        upper = ((own >> j) & 1) == 1
+        bucket = jnp.where(upper, inbox[s, j, h].astype(jnp.float32), 0.0)
+        at = h * STRIDE + first_level + j
+        return w_rows[:, at : at + 1] * dot32(q, bucket.astype(jnp.bfloat16))
+
+    def far_early(s, span):
+        at_span = pl.ds(pl.multiple_of(span * SPAN, SPAN), SPAN)
         w_rows = weights[s, at_span, :]
         for h in range(heads):
             cols = slice(h * head_size, (h + 1) * head_size)
@@ -177,11 +180,21 @@
                 earlier = jnp.where(span > j, states[s, j, h], 0.0).astype(jnp.bfloat16)
                 at = h * STRIDE + lchunk + 1
                 acc = acc + w_rows[:, at : at + 1] * dot32(q, earlier)
-            for j in range(seq_bits):
-                upper = ((own >> j) & 1) == 1
-                bucket = jnp.where(upper, inbox[s, j, h].astype(jnp.float32), 0.0)
-                at = h * STRIDE + first_level + j
-                acc = acc + w_rows[:, at : at + 1] * dot32(q, bucket.astype(jnp.bfloat16))
+            for j in range(seq_bits - 1):
+                acc = acc + bucket_part(s, h, j, q, w_rows)
+            near[s, at_span, cols] = acc
+
+    def far_last(s, span):
+        base_row = span * SPAN
+        at_span = pl.ds(pl.multiple_of(base_row, SPAN), SPAN)
+        first = own * block_len + base_row
+        valid = first + lax.broadcasted_iota(jnp.int32, (SPAN, 1), 0) < lengths_ref[s]
+        w_rows = weights[s, at_span, :]
+        for h in range(heads):
+            cols = slice(h * head_size, (h + 1) * head_size)
+            base = h * 3 * head_size
+            q = qkv[s, at_span, base : base + head_size]
+            acc = near[s, at_span, cols] + bucket_part(s, h, seq_bits - 1, q, w_rows)
             acc = acc * lax.rsqrt(jnp.mean(acc * acc, -1, keepdims=True) + 1e-06)
             out_ref[s, at_span, cols] = jnp.where(valid, acc, 0.0).astype(jnp.bfloat16)
 
@@ -206,13 +219,18 @@
                     @pl.when(last_shard(span) == groups - 1)
                     def _():
                         near_head(s, span, h)
+            if bit == seq_bits - 1:
+                @pl.loop(0, span_count)
+                def _(span):
+                    far_early(s, span)
+
             exchange(s, bit).wait_recv()
             if bit < seq_bits - 1:
                 total[...] = total[...] + inbox[s, bit].astype(jnp.float32)
 
         @pl.loop(0, span_count)
         def _(span):
-            far_span(s, span)
+            far_last(s, span)
 
     @pl.loop(0, batch)
     def _(s):

time: 164 us -> 163 us (level)
  Pallas kernels: 160 us -> 158 us
    pallas_call x1, Pallas kernels: 160 us -> 158 us  [on_device(): pl.pallas_call(functools.partial(kernel, (heads, head_size, groups, seq_b...]
where the time goes in v4:
time: 163 us; the launch traced here: 162 us
  Pallas kernels  158 us (97%)
  local copies, waits for them, and re-layouts  4.49 us (3%)
    pallas_call x1, Pallas kernels, on_device(): pl.pallas_call(functools.partial(kernel, (heads, head_size, groups, seq_b...  158 us

profile of v4, /device:TPU:0, one launch (start us, length us, event | category | flops | bytes accessed | tf_op | source)
XLA Modules:
  0.0 162.3 jit_solution(3887308548773502873)
XLA Ops:
  0.0 0.8 pad.4
  0.8 0.7 reshape.3.table_ref
  1.4 157.8 %attend.1 = bf16[2,1024,512]{2,1,0:T(8,128)(2,1)} custom-call(bf16[2,256,2048]{2,1,0:T(8,128)(2,1)} %tokens_ref.1, f32[1,2048]{1,0:T(1,128)} %bitcast.1, bf16[2048,1536]{1,0:T(8,128)(2,1)} %proj_hbm.1, f32[16,128]{1,0:T(8,128)} %reshape.3.table_ref, s32[2,1024]{1,0:T(2,128)} %index_ref.1, s32[2]{0:T(128)} %lengths_ref.1), custom_call_target="tpu_custom_call" | custom-call | tf_op jit(solution)/shard_map/attend/pallas_call | solution.py:311
  159.2 3.0 %copy.8 = bf16[2,1024,512]{2,1,0:T(8,128)(2,1)} copy(bf16[2,1024,512]{2,1,0:T(8,128)(2,1)} %attend.1) | data formatting | bytes 4194304
